TPU v7x, 1024 devices: a whole 4x4x32 slice. The times are simulated.
1024 devices in a mesh: dp: 32 (over z), expert: 32 (over x, y, core).
Axes of the slice: x: 4, y: 4, z: 32, core: 2. Of those that a mesh axis runs over, the one named last changes fastest.
Arguments:
- tokens: bfloat16 [32, 4096, 2048], P('expert', 'dp'), may hold values from -12 to 12
- routes: int32 [32, 4096, 2], P('expert', 'dp'), may hold values from 0 to 31, all different within a row; in each aligned block of 128 rows (0 to 127, 128 to 255, ..., all dimensions but the last counted through in order) at most 10 rows name the same one
- gate_code: int32 [32, 4096, 2], P('expert', 'dp'), may hold values from 0 to 15
- gate_table: float32 [16], replicated, may hold values from 0.1 to 1
- w_gate: bfloat16 [32, 2048, 704], P('expert'), may hold values from -0.125 to 0.125
- w_up: bfloat16 [32, 2048, 704], P('expert'), may hold values from -0.125 to 0.125
- w_down: bfloat16 [32, 704, 2048], P('expert'), may hold values from -0.7 to 0.7
- norm_gain: float32 [2048], replicated, may hold values from 0.25 to 1.75
Outputs:
- relaid_out: bfloat16 [32, 4096, 2048], P('expert', None, 'dp')
Inputs may be any that keep to these rules, and one draw needn't show every extreme that they name: Within the 128 tokens of one device (aligned blocks of positions) no expert is named by more than 10 routes, a bound that some block reaches; a token's two experts differ.
All inputs are finite; a program needn't handle non-finite values.
Results may differ from a plain program's by a relative error of at most 0.0064.
Values may be sent and summed in bfloat16 or wider, within the bound.
A program may use at most 32 MiB of HBM per device.

v0:
```python
import jax
import jax.numpy as jnp
from jax import lax
from jax.sharding import PartitionSpec as P

epsilon = 1e-06


def expert_ffn(slot_block, w_gate, w_up, w_down):
    shape_in = slot_block.shape
    flat_rows = slot_block.reshape(-1, shape_in[-1])
    gate_act = jnp.dot(flat_rows, w_gate[0], preferred_element_type=jnp.float32)
    up_act = jnp.dot(flat_rows, w_up[0], preferred_element_type=jnp.float32)
    hidden = (jax.nn.silu(gate_act) * up_act).astype(jnp.bfloat16)
    result = jnp.dot(hidden, w_down[0], preferred_element_type=jnp.float32).astype(jnp.bfloat16)
    return result.reshape(shape_in)


def lookup(codes, gate_table):
    levels = gate_table.shape[0]
    match = codes[:, None] == jnp.arange(levels, dtype=jnp.int32)[None, :]
    return jnp.sum(jnp.where(match, gate_table[None, :], 0.0), axis=1)


def combine_pairs(outputs, weights):
    combined = outputs[:, 0] * weights[:, 0:1] + outputs[:, 1] * weights[:, 1:2]
    rounded = lax.optimization_barrier(combined.astype(jnp.bfloat16))
    return rounded.astype(jnp.float32)


def local(tokens, routes, gate_code, gate_table, w_gate, w_up, w_down, norm_gain):
    own_rows = tokens[0]
    tok_count, feat_width = own_rows.shape
    experts = w_gate.shape[0] * lax.axis_size("expert")
    capacity = 5 * tok_count // (2 * experts)
    route_ids = routes[0].reshape(-1)
    onehot = (route_ids[:, None] == jnp.arange(experts, dtype=jnp.int32)[None, :]).astype(jnp.int32)
    slot_pos = jnp.sum((jnp.cumsum(onehot, axis=0) - onehot) * onehot, axis=1)
    position = route_ids * capacity + slot_pos
    owner_row = (
        jnp.zeros((experts * capacity,), jnp.int32)
        .at[position]
        .set(jnp.arange(2 * tok_count, dtype=jnp.int32) // 2)
    )
    filled = jnp.zeros((experts * capacity,), jnp.bool_).at[position].set(True)
    buffer = jnp.where(filled[:, None], own_rows[owner_row], jnp.zeros((), jnp.bfloat16))
    buffer = buffer.reshape(experts, capacity, feat_width)
    level_ids = gate_code[0].reshape(-1)
    received = lax.all_to_all(buffer, "expert", split_axis=0, concat_axis=0, tiled=True)
    expert_out = expert_ffn(received, w_gate, w_up, w_down)
    returned = lax.all_to_all(expert_out, "expert", split_axis=0, concat_axis=0, tiled=True)
    outputs = (
        returned.reshape(-1, feat_width)[position]
        .astype(jnp.float32)
        .reshape(tok_count, 2, feat_width)
    )
    weights = lookup(level_ids, gate_table).reshape(tok_count, 2)
    widened = combine_pairs(outputs, weights)
    inv_rms = lax.rsqrt(jnp.mean(widened * widened, axis=1, keepdims=True) + epsilon)
    normed = (widened * inv_rms * norm_gain[None, :]).astype(jnp.bfloat16)
    relaid = lax.all_to_all(normed, "dp", split_axis=1, concat_axis=0, tiled=True)
    return relaid[None]


def solution(mesh):
    in_specs = (
        P("expert", "dp", None),
        P("expert", "dp", None),
        P("expert", "dp", None),
        P(),
        P("expert", None, None),
        P("expert", None, None),
        P("expert", None, None),
        P(),
    )
    out_specs = P("expert", None, "dp")
    return jax.shard_map(local, mesh=mesh, in_specs=in_specs, out_specs=out_specs, check_vma=False)
```

profile of v0, /device:TPU:1, one launch (start us, length us, event | category | flops | bytes accessed | tf_op | source)
XLA Modules:
  0.0 222.4 jit_solution(13236783695997548187)
XLA Ops:
  0.0 0.9 copy.27
  1.1 0.1 eq.40
  1.2 0.7 broadcast_multiply_fusion
  1.9 0.6 reduce-window.6
  2.5 0.2 slice_reduce_fusion.2
  2.9 0.1 mul.67
  3.1 1.4 scatter_custom_fusion.1
  4.6 3.0 %gather_fusion = bf16[320,2048]{1,0:T(8,128)(2,1)} fusion(bf16[128,2048]{1,0:T(8,128)(2,1)S(1)} %bitcast.55, s32[1024]{0:T(1024)S(1)} %pad_clamp_fusion.1), kind=kCustom, calls=%fused_computation | custom fusion | bytes 2622720 | tf_op jit(solution)/shard_map/gather | solution.py:46
  7.6 3.3 %gather.9 = bf16[32,10,2048]{2,1,0:T(8,128)(2,1)} reshape(bf16[320,2048]{1,0:T(8,128)(2,1)} %gather_fusion) | data formatting | bytes 2621440 | tf_op jit(solution)/shard_map/gather | solution.py:46
  10.9 1.5 scatter_custom_fusion
  12.5 1.8 broadcast_select_fusion
  14.4 45.7 %all_to_all.26 = bf16[32,10,2048]{2,1,0:T(8,128)(2,1)} all-to-all(bf16[32,10,2048]{2,1,0:T(8,128)(2,1)S(1)} %broadcast_select_fusion), channel_id=1, replica_groups=mesh['dp'=32,'expert'=32] {'expert'}, dimensions={0} | all-to-all | bytes 2621440 | tf_op jit(solution)/shard_map/all_to_all | solution.py:49
  60.1 3.6 %reshape.85 = bf16[320,2048]{1,0:T(8,128)(2,1)} reshape(bf16[32,10,2048]{2,1,0:T(8,128)(2,1)} %all_to_all.26) | data formatting | bytes 2621440 | tf_op jit(solution)/shard_map/reshape | solution.py:11
  63.7 4.4 %fusion.4 = f32[320,704]{1,0:T(8,128)} fusion(bf16[320,2048]{1,0:T(8,128)(2,1)} %reshape.85, bf16[1,2048,704]{1,2,0:T(8,128)(2,1)} %param.12), kind=kOutput, calls=%fused_computation.8 | convolution fusion | flops 922746880 | bytes 5095424 | tf_op jit(solution)/shard_map/dot_general | solution.py:12
  68.1 6.1 %fusion.6 = bf16[320,2048]{1,0:T(8,128)(2,1)} fusion(bf16[1,704,2048]{2,1,0:T(8,128)(2,1)S(1)} %copy-done, bf16[320,2048]{1,0:T(8,128)(2,1)} %reshape.85, bf16[1,2048,704]{1,2,0:T(8,128)(2,1)} %param.13, f32[320,704]{1,0:T(8,128)} %fusion.4), kind=kOutput, calls=%fused_computation.10 | convolution fusion | flops 1847500800 | bytes 9289728 | tf_op jit(solution)/shard_map/dot_general | solution.py:15
  74.3 3.3 %reshape.86 = bf16[32,10,2048]{2,1,0:T(8,128)(2,1)} reshape(bf16[320,2048]{1,0:T(8,128)(2,1)} %fusion.6) | data formatting | bytes 2621440 | tf_op jit(solution)/shard_map/reshape | solution.py:16
  77.6 4.9 %all-to-all-start.1 = ((bf16[32,10,2048]{2,1,0:T(8,128)(2,1)}), bf16[32,10,2048]{2,1,0:T(8,128)(2,1)}, u32[]{:S(2)}, u32[]{:S(2)}) async-start(bf16[32,10,2048]{2,1,0:T(8,128)(2,1)} %reshape.86), calls=%async_computation.1 | async-start | bytes 4194304 | tf_op jit(solution)/shard_map/all_to_all | solution.py:51
  82.6 0.1 eq.48
  83.0 0.2 slice_reduce_fusion.1
  83.2 27.5 %all-to-all-done.1 = bf16[32,10,2048]{2,1,0:T(8,128)(2,1)} async-done(((bf16[32,10,2048]{2,1,0:T(8,128)(2,1)}), bf16[32,10,2048]{2,1,0:T(8,128)(2,1)}, u32[]{:S(2)}, u32[]{:S(2)}) %all-to-all-start.1) | async-done | bytes 1310752 | tf_op jit(solution)/shard_map/all_to_all | solution.py:51
  110.7 3.6 %reshape.87 = bf16[320,2048]{1,0:T(8,128)(2,1)} reshape(bf16[32,10,2048]{2,1,0:T(8,128)(2,1)} %all-to-all-done.1) | data formatting | bytes 2621440 | tf_op jit(solution)/shard_map/reshape | solution.py:53
  114.3 4.8 %gather_fusion.1 = bf16[256,2048]{1,0:T(8,128)(2,1)} fusion(bf16[320,2048]{1,0:T(8,128)(2,1)} %reshape.87, s32[1024]{0:T(1024)S(1)} %pad_clamp_fusion), kind=kCustom, calls=%fused_computation.1 | custom fusion | bytes 2098176 | tf_op jit(solution)/shard_map/gather | solution.py:53
  119.1 3.4 %reshape.89 = f32[128,2,2048]{2,1,0:T(2,128)} reshape(bf16[256,2048]{1,0:T(8,128)(2,1)} %gather_fusion.1) | data formatting | bytes 3145728 | tf_op jit(solution)/shard_map/convert_element_type | solution.py:54
  122.5 5.7 %fusion.32 = (f32[128,1,2048]{2,1,0:T(1,128)}, f32[128,1,2048]{2,1,0:T(1,128)}) fusion(f32[128,2,2048]{2,1,0:T(2,128)} %reshape.89), kind=kLoop, calls=%fused_computation.52 | loop fusion | bytes 4194304 | tf_op jit(solution)/shard_map/slice | solution.py:26
  128.2 3.6 %copy.34 = f32[128,1,2048]{0,2,1:T(8,128)} copy(f32[128,1,2048]{2,1,0:T(1,128)} %get-tuple-element.7) | data formatting | bytes 2097152
  131.8 3.6 %copy.35 = f32[128,1,2048]{0,2,1:T(8,128)} copy(f32[128,1,2048]{2,1,0:T(1,128)} %get-tuple-element.8) | data formatting | bytes 2097152
  135.4 1.7 fusion.19
  137.1 0.3 fusion.15
  137.4 0.3 fusion.17
  137.7 83.3 %all_to_all.27 = bf16[128,32,64]{0,2,1:T(8,128)(2,1)S(1)} all-to-all(bf16[128,32,64]{0,2,1:T(8,128)(2,1)S(1)} %bitcast.56), channel_id=1, replica_groups=mesh['dp'=32,'expert'=32] {'dp'}, dimensions={1} | all-to-all | bytes 1048576 | tf_op jit(solution)/shard_map/all_to_all | solution.py:61
  221.0 0.3 copy.33
  221.4 1.0 broadcast_in_dim.55
  (27 shorter events, 0.9 us)
Async XLA Ops:
  0.0 68.1 %copy-start = (bf16[1,704,2048]{2,1,0:T(8,128)(2,1)S(1)}, bf16[1,704,2048]{2,1,0:T(8,128)(2,1)}, u32[]{:S(2)}) copy-start(bf16[1,704,2048]{2,1,0:T(8,128)(2,1)} %param.14) | copy-start | bytes 8650756
  0.0 4.5 %copy-start.1 = (bf16[1,128,2048]{2,1,0:T(8,128)(2,1)S(1)}, bf16[1,128,2048]{2,1,0:T(8,128)(2,1)}, u32[]{:S(2)}) copy-start(bf16[1,128,2048]{2,1,0:T(8,128)(2,1)} %param.8) | copy-start | bytes 1572868
  77.6 4.9 %copy-start.3 = (s32[1,128,2]{1,2,0:T(2,128)S(1)}, s32[1,128,2]{1,2,0:T(2,128)}, u32[]{:S(2)}) copy-start(s32[1,128,2]{1,2,0:T(2,128)} %param.10) | copy-start | bytes 3076
  77.6 5.1 %copy-start.4 = (f32[16]{0:T(128)S(1)}, f32[16]{0:T(128)}, u32[]{:S(2)}) copy-start(f32[16]{0:T(128)} %param.11) | copy-start | bytes 196
  77.6 33.0 %all-to-all-start.1 = ((bf16[32,10,2048]{2,1,0:T(8,128)(2,1)}), bf16[32,10,2048]{2,1,0:T(8,128)(2,1)}, u32[]{:S(2)}, u32[]{:S(2)}) async-start(bf16[32,10,2048]{2,1,0:T(8,128)(2,1)} %reshape.86), calls=%async_computation.1 | async-start | bytes 4194304 | tf_op jit(solution)/shard_map/all_to_all | solution.py:51
  135.4 2.0 copy-start.2
where the time goes:
time: 223 us; the launch traced here: 222 us
  blocking collectives  129 us (58%)
  local copies, waits for them, and re-layouts  44.6 us (20%)
  waiting for transfers between devices  27.5 us (12%)
  matrix products  10.6 us (5%)
  other arithmetic  5.66 us (3%)
  starting transfers between devices  4.86 us (2%)
    all_to_all x1, blocking collectives, local(): lax.all_to_all(normed, 'dp', split_axis=1, concat_axis=0, tiled=True)  83.3 us
    all_to_all x1, blocking collectives, local(): lax.all_to_all(buffer, 'expert', split_axis=0, concat_axis=0, tiled=True)  45.7 us
    all_to_all x1, waiting for transfers between devices, local(): lax.all_to_all(expert_out, 'expert', split_axis=0, concat_axis=0, tiled=T...  27.5 us
    unnamed x14, local copies, waits for them, and re-layouts  8.27 us
    gather x2, local copies, waits for them, and re-layouts, local(): own_rows[owner_row]  6.38 us
    dot_general x1, matrix products, expert_ffn(): jnp.dot(hidden, w_down[0], preferred_element_type=jnp.float32)  6.14 us
    slice x2, local copies, waits for them, and re-layouts, combine_pairs(): combined = outputs[:, 0] * weights[:, 0:1] + outputs[:, 1] * weights[:, 1:2]  5.84 us
    all_to_all x1, starting transfers between devices, local(): lax.all_to_all(expert_out, 'expert', split_axis=0, concat_axis=0, tiled=T...  4.86 us
  transfers between devices with their start and end apart: 1, of which 1 were waited for; matrix products, arithmetic and copies ran while one was open for 0% of the time, Pallas kernels for 0%

commit v1 on v0

v1 whole, which is shorter than its diff:
```python
import functools

import jax
import jax.numpy as jnp
from jax import lax
from jax.experimental import pallas as pl
from jax.experimental.pallas import tpu as pltpu
from jax.sharding import PartitionSpec as P

epsilon = 1e-06
MESH = pl.DeviceIdType.MESH
BF16 = jnp.bfloat16
F32 = jnp.float32

N = 32
TOK = 128
D = 2048
FF = 704
MAIN = 8
REST = 2
QUAD = 256
CHUNKS = 5


def drain(ref, count, sem):
    pltpu.make_async_copy(ref.at[pl.ds(0, count)], ref.at[pl.ds(0, count)], sem).wait()


def iota(shape, dim):
    return lax.broadcasted_iota(jnp.int32, shape, dim)


def onehot(cond):
    return jnp.where(cond, 1.0, 0.0).astype(BF16)


def slots_of(routes):
    own = [jnp.where(iota((N, TOK), 0) == routes[k : k + 1], 1.0, 0.0) for k in range(2)]
    before = jnp.where(iota((TOK, TOK), 0) < iota((TOK, TOK), 1), 1.0, 0.0).astype(BF16)
    earlier = [jnp.dot(o.astype(BF16), before, preferred_element_type=F32) for o in own]
    first = jnp.sum(own[0], axis=1, keepdims=True)
    rank0 = jnp.sum(own[0] * earlier[0], axis=0, keepdims=True)
    rank1 = jnp.sum(own[1] * (earlier[1] + first), axis=0, keepdims=True)
    return [rank0.astype(jnp.int32), rank1.astype(jnp.int32)]


def kernel(
    tok_hbm, routes_hbm, codes_hbm, table_ref, wg_hbm, wu_hbm, wd_hbm, gain_hbm, out_ref,
    tok, routes, codes, gain, wg, wu, wd,
    send, recv, rest_x, gate, up, hid, mix, ret_s, ret_r, z_s, z_r, inv_s, inv_r, ssq,
    load_sem, send_sem, recv_sem, rsend_sem, rrecv_sem, zsend_sem, zrecv_sem, isend_sem, irecv_sem,
):
    z = lax.axis_index("dp")
    e = lax.axis_index("expert")

    bar = pltpu.get_barrier_semaphore()

    @pl.loop(1, N)
    def _(d):
        pl.semaphore_signal(bar, 1, device_id={"expert": e ^ d}, device_id_type=MESH)

    @pl.loop(1, N)
    def _(d):
        pl.semaphore_signal(bar, 1, device_id={"dp": (z + d) % N}, device_id_type=MESH)

    loads = [
        pltpu.make_async_copy(a, b, load_sem.at[i])
        for i, (a, b) in enumerate(
            [(tok_hbm, tok), (routes_hbm, routes), (codes_hbm, codes), (gain_hbm, gain), (wg_hbm, wg), (wu_hbm, wu), (wd_hbm, wd)]
        )
    ]
    for load in loads:
        load.start()
    for load in loads[:3]:
        load.wait()

    to = [routes[k : k + 1, :] for k in range(2)]
    rank = slots_of(routes[...])
    main_at = [jnp.where(r < MAIN, t * MAIN + r, -1) for t, r in zip(to, rank)]
    rest_at = [jnp.where(r >= MAIN, t * REST + r - MAIN, -1) for t, r in zip(to, rank)]
    back_at = [t * 16 + r for t, r in zip(to, rank)]

    rows = iota((N * MAIN, TOK), 0)
    pick = onehot((rows == main_at[0]) | (rows == main_at[1]))
    for c in range(4):
        both = jnp.dot(pick, tok[:, c * 512 : (c + 1) * 512], preferred_element_type=F32)
        folded = jnp.stack([both[:, :256].reshape(N, 8, 256), both[:, 256:].reshape(N, 8, 256)], axis=1)
        send[c * N : (c + 1) * N] = folded.reshape(N, 16, 256).astype(BF16)
    rows = iota((N * 16, TOK), 0)
    held = (rows // 8 == rest_at[0]) | (rows // 8 == rest_at[1])
    total = jnp.zeros((N * 16, 256), F32)
    for q in range(8):
        part = onehot(held & (rows % 8 == q))
        total += jnp.dot(part, tok[:, q * 256 : (q + 1) * 256], preferred_element_type=F32)
    send[4 * N : 5 * N] = total.reshape(N, 16, 256).astype(BF16)

    pl.semaphore_wait(bar, 2 * (N - 1))

    for c in (4, 0, 1, 2, 3):

        @pl.loop(1, N)
        def _(d):
            t = e ^ d
            pltpu.make_async_remote_copy(
                send.at[c * N + t], recv.at[c * N + e], send_sem, recv_sem.at[c], device_id={"expert": t}, device_id_type=MESH
            ).start()

        recv[c * N + e] = send[c * N + e]

    weight = [jnp.zeros((1, TOK), F32) for _ in range(2)]
    for k in range(2):
        for level in range(16):
            weight[k] = jnp.where(codes[k : k + 1, :] == level, table_ref[level], weight[k])
    rows = iota((N * 16, TOK), 0)
    wide = jnp.where(rows == back_at[0], weight[0], 0.0) + jnp.where(rows == back_at[1], weight[1], 0.0)
    wide = wide.T
    high = wide.astype(BF16)
    mix[:TOK] = high
    mix[TOK:] = (wide - high.astype(F32)).astype(BF16)
    ssq[...] = jnp.zeros_like(ssq)

    for load in loads[4:6]:
        load.wait()
    drain(recv, N - 1, recv_sem.at[4])
    at = iota((N * 16, N * 16), 0)
    unfold = onehot(iota((N * 16, N * 16), 1) == (at % 64) * 8 + at // 64)
    rest_x[...] = jnp.dot(unfold, recv[4 * N : 5 * N].reshape(N * 16, 256), preferred_element_type=F32).astype(BF16)
    for c in range(4):
        drain(recv, N - 1, recv_sem.at[c])
        halves = [
            jnp.concatenate(
                [recv[c * N : (c + 1) * N, h * 8 : (h + 1) * 8].reshape(N * 8, 256), rest_x[(2 * c + h) * 64 : (2 * c + h + 1) * 64]],
                axis=0,
            )
            for h in range(2)
        ]
        x = jnp.concatenate(halves, axis=1)
        for w, acc in ((wg, gate), (wu, up)):
            part = lax.dot_general(x, w[:, c * 512 : (c + 1) * 512], (((1,), (1,)), ((), ())), preferred_element_type=F32)
            if c == 0:
                acc[...] = part
            else:
                acc[...] += part
    g = gate[...]
    h = (g / (1.0 + jnp.exp(-g)) * up[...]).astype(BF16)
    hid[: N * 8] = h[: N * 8]
    spread = onehot(iota((N * 8, 64), 1) == (iota((N * 8, 64), 0) // 8) * 2 + iota((N * 8, 64), 0) % 8)
    spread = jnp.where(iota((N * 8, 64), 0) % 8 < 2, spread, jnp.zeros((), BF16))
    hid[N * 8 :] = jnp.dot(spread, h[N * 8 :], preferred_element_type=F32).astype(BF16)
    loads[6].wait()
    loads[3].wait()

    def quad_of(k):
        far = (k + 1) // 2
        return (z // 4 + 4 + jnp.where(k % 2 == 1, -far, far)) % 8

    def expert_part(k):
        quad = quad_of(k)
        cols = pl.ds(pl.multiple_of(quad * QUAD, QUAD), QUAD)
        out = jnp.dot(hid[...], wd[:, cols], preferred_element_type=F32)
        both = jnp.stack([out[: N * 8].reshape(N, 8, QUAD), out[N * 8 :].reshape(N, 8, QUAD)], axis=1)
        ret_s[pl.ds(k * N, N)] = both.reshape(N, 16, QUAD).astype(BF16)

        @pl.loop(1, N)
        def _(d):
            t = e ^ d
            pltpu.make_async_remote_copy(
                ret_s.at[k * N + t], ret_r.at[k * N + e], rsend_sem, rrecv_sem.at[k], device_id={"expert": t}, device_id_type=MESH
            ).start()

        ret_r[k * N + e] = ret_s[k * N + e]

    def home_part(k):
        quad = quad_of(k)
        drain(ret_r, N - 1, rrecv_sem.at[k])
        block = ret_r[pl.ds(k * N, N)].reshape(N * 16, QUAD)
        pair = jnp.dot(mix[...], block, preferred_element_type=F32)
        comb = (pair[:TOK] + pair[TOK:]).astype(BF16).astype(F32).T
        ssq[...] += jnp.sum(comb * comb, axis=0, keepdims=True)
        base = pl.multiple_of(quad * QUAD, QUAD)
        z_s[pl.ds(base, QUAD)] = comb.astype(BF16)

        @pl.loop(0, 4)
        def _(b):
            t = quad * 4 + b

            @pl.when(t != z)
            def _():
                pltpu.make_async_remote_copy(
                    z_s.at[pl.ds(pl.multiple_of(t * 64, 64), 64)], z_r.at[z], zsend_sem, zrecv_sem, device_id={"dp": t}, device_id_type=MESH
                ).start()

    expert_part(0)

    @pl.loop(1, 8)
    def _(k):
        expert_part(k)
        home_part(k - 1)

    home_part(7)

    inv_s[...] = lax.rsqrt(ssq[...] * (1.0 / D) + epsilon)

    @pl.loop(1, N)
    def _(d):
        pltpu.make_async_remote_copy(
            inv_s, inv_r.at[z], isend_sem, irecv_sem, device_id={"dp": (z + d) % N}, device_id_type=MESH
        ).start()

    inv_r[z] = inv_s[...]
    z_r[z] = z_s[pl.ds(pl.multiple_of(z * 64, 64), 64)]

    line = jnp.broadcast_to(gain[pl.ds(z // 2, 1), :], (64, 128))
    mine = iota((64, 128), 1) == iota((64, 128), 0) + 64 * (z % 2)
    column = jnp.sum(jnp.where(mine, line, 0.0), axis=1, keepdims=True)

    drain(send, CHUNKS * (N - 1), send_sem)
    drain(ret_s, 8 * (N - 1), rsend_sem)
    drain(z_s, (N - 1) * 64, zsend_sem)
    drain(inv_r, N - 1, isend_sem)
    drain(z_r, N - 1, zrecv_sem)
    drain(inv_r, N - 1, irecv_sem)
    for s in range(N):
        out_ref[:, s * TOK : (s + 1) * TOK] = (z_r[s].astype(F32) * inv_r[s] * column).astype(BF16)


def local(tokens, routes, gate_code, gate_table, w_gate, w_up, w_down, norm_gain):
    anywhere = pl.BlockSpec(memory_space=pl.ANY)
    dma = pltpu.SemaphoreType.DMA
    relaid = pl.pallas_call(
        kernel,
        out_shape=jax.ShapeDtypeStruct((D // N, N * TOK), BF16),
        in_specs=[anywhere] * 3 + [pl.BlockSpec(memory_space=pltpu.SMEM)] + [anywhere] * 4,
        out_specs=pl.BlockSpec(memory_space=pltpu.VMEM),
        scratch_shapes=[
            pltpu.VMEM((TOK, D), BF16),
            pltpu.VMEM((2, TOK), jnp.int32),
            pltpu.VMEM((2, TOK), jnp.int32),
            pltpu.VMEM((16, 128), F32),
            pltpu.VMEM((FF, D), BF16),
            pltpu.VMEM((FF, D), BF16),
            pltpu.VMEM((FF, D), BF16),
            pltpu.VMEM((CHUNKS * N, 16, 256), BF16),
            pltpu.VMEM((CHUNKS * N, 16, 256), BF16),
            pltpu.VMEM((N * 16, 256), BF16),
            pltpu.VMEM((320, FF), F32),
            pltpu.VMEM((320, FF), F32),
            pltpu.VMEM((N * 16, FF), BF16),
            pltpu.VMEM((2 * TOK, N * 16), BF16),
            pltpu.VMEM((8 * N, 16, QUAD), BF16),
            pltpu.VMEM((8 * N, 16, QUAD), BF16),
            pltpu.VMEM((D, TOK), BF16),
            pltpu.VMEM((N, 64, TOK), BF16),
            pltpu.VMEM((1, TOK), F32),
            pltpu.VMEM((N, 1, TOK), F32),
            pltpu.VMEM((1, TOK), F32),
            dma((7,)), dma, dma((CHUNKS,)), dma, dma((8,)), dma, dma, dma, dma,
        ],
        compiler_params=pltpu.CompilerParams(collective_id=0, has_side_effects=True, vmem_limit_bytes=48 << 20),
        cost_estimate=pl.CostEstimate(flops=3 << 30, bytes_accessed=10 << 20, transcendentals=320 * FF),
    )(
        tokens[0],
        routes[0].T,
        gate_code[0].T,
        gate_table,
        jnp.swapaxes(w_gate[0], 0, 1),
        jnp.swapaxes(w_up[0], 0, 1),
        w_down[0],
        norm_gain.reshape(16, 128),
    )
    return relaid.T[None]


def solution(mesh):
    in_specs = (
        P("expert", "dp", None),
        P("expert", "dp", None),
        P("expert", "dp", None),
        P(),
        P("expert", None, None),
        P("expert", None, None),
        P("expert", None, None),
        P(),
    )
    out_specs = P("expert", None, "dp")
    return jax.shard_map(local, mesh=mesh, in_specs=in_specs, out_specs=out_specs, check_vma=False)
```

time: 223 us -> 119 us (0.53)
  blocking collectives: 129 us -> 0 us
  Pallas kernels: 0 us -> 112 us
  local copies, waits for them, and re-layouts: 44.6 us -> 6.36 us
  waiting for transfers between devices: 27.5 us -> 0 us
  matrix products: 10.6 us -> 0 us
  other arithmetic: 5.66 us -> 0 us
  starting transfers between devices: 4.86 us -> 0 us
    all_to_all x2 -> x0, blocking collectives: 129 us -> none  [the longest x1 83.3 us: local(): lax.all_to_all(normed, 'dp', split_axis=1, concat_axis=0, tiled=True)]
    pallas_call x0 -> x1, Pallas kernels: none -> 112 us  [local(): pl.pallas_call(kernel, out_shape=jax.ShapeDtypeStruct((D // N, N * TOK),...]
    all_to_all x1 -> x0, waiting for transfers between devices: 27.5 us -> none  [local(): lax.all_to_all(expert_out, 'expert', split_axis=0, concat_axis=0, tiled=T...]
    gather x3 -> x0, local copies, waits for them, and re-layouts: 11.2 us -> none  [the longest x2 6.38 us: local(): own_rows[owner_row]]
    reshape x4 -> x0, local copies, waits for them, and re-layouts: 10.7 us -> none  [the longest x1 3.61 us: local(): returned.reshape(-1, feat_width)[position].astype(jnp.float32)]
    dot_general x2 -> x0, matrix products: 10.6 us -> none  [the longest x1 6.14 us: expert_ffn(): jnp.dot(hidden, w_down[0], preferred_element_type=jnp.float32)]
    slice x3 -> x0, local copies, waits for them, and re-layouts: 6.03 us -> none  [the longest x2 5.84 us: combine_pairs(): combined = outputs[:, 0] * weights[:, 0:1] + outputs[:, 1] * weights[:, 1:2]]
    all_to_all x1 -> x0, starting transfers between devices: 4.86 us -> none  [local(): lax.all_to_all(expert_out, 'expert', split_axis=0, concat_axis=0, tiled=T...]
  transfers between devices with their start and end apart: 1 -> 0, of which waited for: 1 -> 0; matrix products, arithmetic and copies ran while one was open for 0% -> 0% of each run, Pallas kernels for 0% -> 0%
where the time goes in v1:
time: 119 us; the launch traced here: 118 us
  Pallas kernels  112 us (94%)
  local copies, waits for them, and re-layouts  6.36 us (5%)
    pallas_call x1, Pallas kernels, local(): pl.pallas_call(kernel, out_shape=jax.ShapeDtypeStruct((D // N, N * TOK),...  112 us
    unnamed x13, local copies, waits for them, and re-layouts  6.36 us

profile of v1, /device:TPU:1, one launch (start us, length us, event | category | flops | bytes accessed | tf_op | source)
XLA Modules:
  0.0 118.4 jit_solution(9224890309319975200)
XLA Ops:
  0.0 0.0 copy-start
  0.0 1.8 %copy-done = bf16[1,2048,704]{1,2,0:T(8,128)(2,1)S(1)} copy-done((bf16[1,2048,704]{1,2,0:T(8,128)(2,1)S(1)}, bf16[1,2048,704]{1,2,0:T(8,128)(2,1)}, u32[]{:S(2)}) %copy-start) | copy-done | bytes 2883608
  1.8 0.0 copy-start.1
  1.8 1.0 copy-done.1
  2.9 0.0 copy-start.2
  2.9 0.7 copy-done.2
  3.6 0.0 copy-start.3
  3.6 0.7 copy-done.3
  4.2 0.0 copy-start.4
  4.2 0.7 copy-done.4
  4.9 0.0 copy-start.5
  4.9 0.7 copy-done.5
  5.6 112.0 %shard_map.82 = bf16[64,4096]{1,0:T(8,128)(2,1)S(1)} custom-call(bf16[128,2048]{1,0:T(8,128)(2,1)S(1)} %bitcast.20, s32[2,128]{1,0:T(2,128)S(1)} %bitcast.22, s32[2,128]{1,0:T(2,128)S(1)} %bitcast.23, f32[16]{0:T(128)S(1)} %copy-done.5, bf16[704,2048]{1,0:T(8,128)(2,1)S(1)} %bitcast.19, bf16[704,2048]{1,0:T(8,128)(2,1)} %bitcast.24, ...), custom_call_target="tpu_custom_call" | custom-call | flops 3221225472 | bytes 10485760 | tf_op jit(solution)/shard_map/pallas_call | solution.py:230
  117.6 0.8 copy.10
Async XLA Ops:
  0.0 1.8 %copy-start = (bf16[1,2048,704]{1,2,0:T(8,128)(2,1)S(1)}, bf16[1,2048,704]{1,2,0:T(8,128)(2,1)}, u32[]{:S(2)}) copy-start(bf16[1,2048,704]{1,2,0:T(8,128)(2,1)} %param.12) | copy-start | bytes 8650756
  1.8 1.0 copy-start.1
  2.9 0.7 copy-start.2
  3.6 0.7 copy-start.3
  4.2 0.7 copy-start.4
  4.9 0.7 copy-start.5

commit v2 on v1

--- a/solution.py
+++ b/solution.py
@@ -19,6 +19,8 @@
 MAIN = 8
 REST = 2
 QUAD = 256
+RELAY = 31
+LAG = 2
 CHUNKS = 5
 
 
@@ -47,8 +49,8 @@
 def kernel(
     tok_hbm, routes_hbm, codes_hbm, table_ref, wg_hbm, wu_hbm, wd_hbm, gain_hbm, out_ref,
     tok, routes, codes, gain, wg, wu, wd,
-    send, recv, rest_x, gate, up, hid, mix, ret_s, ret_r, z_s, z_r, inv_s, inv_r, ssq,
-    load_sem, send_sem, recv_sem, rsend_sem, rrecv_sem, zsend_sem, zrecv_sem, isend_sem, irecv_sem,
+    send, recv, rest_x, gate, up, hid, mix, fold, unfold, ret_s, ret_r, back_x, z_s, z_r, inv_s, inv_r, ssq,
+    load_sem, send_sem, recv_sem, rsend_sem, rrecv_sem, zsend_sem, zrecv_sem, isend_sem, irecv_sem, plane_sem, open_sem,
 ):
     z = lax.axis_index("dp")
     e = lax.axis_index("expert")
@@ -57,11 +59,9 @@
 
     @pl.loop(1, N)
     def _(d):
-        pl.semaphore_signal(bar, 1, device_id={"expert": e ^ d}, device_id_type=MESH)
-
-    @pl.loop(1, N)
-    def _(d):
-        pl.semaphore_signal(bar, 1, device_id={"dp": (z + d) % N}, device_id_type=MESH)
+        @pl.when(e ^ d != RELAY)
+        def _():
+            pl.semaphore_signal(bar, 1, device_id={"expert": e ^ d}, device_id_type=MESH)
 
     loads = [
         pltpu.make_async_copy(a, b, load_sem.at[i])
@@ -78,7 +78,6 @@
     rank = slots_of(routes[...])
     main_at = [jnp.where(r < MAIN, t * MAIN + r, -1) for t, r in zip(to, rank)]
     rest_at = [jnp.where(r >= MAIN, t * REST + r - MAIN, -1) for t, r in zip(to, rank)]
-    back_at = [t * 16 + r for t, r in zip(to, rank)]
 
     rows = iota((N * MAIN, TOK), 0)
     pick = onehot((rows == main_at[0]) | (rows == main_at[1]))
@@ -94,7 +93,25 @@
         total += jnp.dot(part, tok[:, q * 256 : (q + 1) * 256], preferred_element_type=F32)
     send[4 * N : 5 * N] = total.reshape(N, 16, 256).astype(BF16)
 
-    pl.semaphore_wait(bar, 2 * (N - 1))
+    at = iota((N * 16, N * 16), 0)
+    unfold[...] = onehot(iota((N * 16, N * 16), 1) == (at % 64) * 8 + at // 64)
+    fold[...] = onehot(iota((N * 16, N * 16), 1) == (at % 8) * 64 + at // 8)
+
+    @pl.when(e != RELAY)
+    def _():
+        pl.semaphore_wait(bar, N - 1)
+
+    @pl.when(e == RELAY - 1)
+    def _():
+        pl.semaphore_signal(plane_sem, 1, device_id={"expert": RELAY}, device_id_type=MESH)
+
+    @pl.when(e == RELAY)
+    def _():
+        pl.semaphore_wait(plane_sem, 1)
+
+        @pl.loop(1, N)
+        def _(d):
+            pl.semaphore_signal(bar, 1, device_id={"dp": (z + d) % N}, device_id_type=MESH)
 
     for c in (4, 0, 1, 2, 3):
 
@@ -111,9 +128,11 @@
     for k in range(2):
         for level in range(16):
             weight[k] = jnp.where(codes[k : k + 1, :] == level, table_ref[level], weight[k])
-    rows = iota((N * 16, TOK), 0)
-    wide = jnp.where(rows == back_at[0], weight[0], 0.0) + jnp.where(rows == back_at[1], weight[1], 0.0)
-    wide = wide.T
+    rows = iota((384, TOK), 0)
+    wide = jnp.zeros((384, TOK), F32)
+    for k in range(2):
+        wide += jnp.where(rows == jnp.where(rank[k] < MAIN, main_at[k], N * MAIN + rest_at[k]), weight[k], 0.0)
+    wide = wide.T[:, :320]
     high = wide.astype(BF16)
     mix[:TOK] = high
     mix[TOK:] = (wide - high.astype(F32)).astype(BF16)
@@ -122,9 +141,7 @@
     for load in loads[4:6]:
         load.wait()
     drain(recv, N - 1, recv_sem.at[4])
-    at = iota((N * 16, N * 16), 0)
-    unfold = onehot(iota((N * 16, N * 16), 1) == (at % 64) * 8 + at // 64)
-    rest_x[...] = jnp.dot(unfold, recv[4 * N : 5 * N].reshape(N * 16, 256), preferred_element_type=F32).astype(BF16)
+    rest_x[...] = jnp.dot(unfold[...], recv[4 * N : 5 * N].reshape(N * 16, 256), preferred_element_type=F32).astype(BF16)
     for c in range(4):
         drain(recv, N - 1, recv_sem.at[c])
         halves = [
@@ -142,11 +159,7 @@
             else:
                 acc[...] += part
     g = gate[...]
-    h = (g / (1.0 + jnp.exp(-g)) * up[...]).astype(BF16)
-    hid[: N * 8] = h[: N * 8]
-    spread = onehot(iota((N * 8, 64), 1) == (iota((N * 8, 64), 0) // 8) * 2 + iota((N * 8, 64), 0) % 8)
-    spread = jnp.where(iota((N * 8, 64), 0) % 8 < 2, spread, jnp.zeros((), BF16))
-    hid[N * 8 :] = jnp.dot(spread, h[N * 8 :], preferred_element_type=F32).astype(BF16)
+    hid[...] = (g / (1.0 + jnp.exp(-g)) * up[...]).astype(BF16)
     loads[6].wait()
     loads[3].wait()
 
@@ -154,26 +167,45 @@
         far = (k + 1) // 2
         return (z // 4 + 4 + jnp.where(k % 2 == 1, -far, far)) % 8
 
-    def expert_part(k):
-        quad = quad_of(k)
-        cols = pl.ds(pl.multiple_of(quad * QUAD, QUAD), QUAD)
-        out = jnp.dot(hid[...], wd[:, cols], preferred_element_type=F32)
-        both = jnp.stack([out[: N * 8].reshape(N, 8, QUAD), out[N * 8 :].reshape(N, 8, QUAD)], axis=1)
-        ret_s[pl.ds(k * N, N)] = both.reshape(N, 16, QUAD).astype(BF16)
+    def columns(quad):
+        return wd[:, pl.ds(pl.multiple_of(quad * QUAD, QUAD), QUAD)]
+
+    def give_back(at, block):
+        ret_s[pl.ds(at * N, N)] = block.reshape(N, 16, 128).astype(BF16)
 
         @pl.loop(1, N)
         def _(d):
             t = e ^ d
             pltpu.make_async_remote_copy(
-                ret_s.at[k * N + t], ret_r.at[k * N + e], rsend_sem, rrecv_sem.at[k], device_id={"expert": t}, device_id_type=MESH
+                ret_s.at[at * N + t], ret_r.at[at * N + e], rsend_sem, rrecv_sem.at[at], device_id={"expert": t}, device_id_type=MESH
             ).start()
 
-        ret_r[k * N + e] = ret_s[k * N + e]
-
-    def home_part(k):
+        ret_r[at * N + e] = ret_s[at * N + e]
+
+    def expert_rest(half):
+        pieces = []
+        for i in range(4):
+            out = jnp.dot(hid[N * MAIN :], columns(quad_of(half * 4 + i)), preferred_element_type=F32).astype(BF16)
+            pieces += [out[:, :128], out[:, 128:]]
+        give_back(8 + half, jnp.dot(fold[...], jnp.concatenate(pieces, axis=0), preferred_element_type=F32))
+
+    def expert_main(k):
+        out = jnp.dot(hid[: N * MAIN], columns(quad_of(k)), preferred_element_type=F32)
+        give_back(k, jnp.stack([out[:, :128].reshape(N, 8, 128), out[:, 128:].reshape(N, 8, 128)], axis=1))
+
+    def home_rest(half):
+        drain(ret_r, N - 1, rrecv_sem.at[8 + half])
+        block = ret_r[pl.ds((8 + half) * N, N)].reshape(N * 16, 128)
+        back_x[...] = jnp.dot(unfold[...], block, preferred_element_type=F32).reshape(8, 64, 128).astype(BF16)
+
+    def home_main(k):
         quad = quad_of(k)
         drain(ret_r, N - 1, rrecv_sem.at[k])
-        block = ret_r[pl.ds(k * N, N)].reshape(N * 16, QUAD)
+        halves = [
+            jnp.concatenate([ret_r[pl.ds(k * N, N), h * 8 : (h + 1) * 8].reshape(N * 8, 128), back_x[2 * (k % 4) + h]], axis=0)
+            for h in range(2)
+        ]
+        block = jnp.concatenate(halves, axis=1)
         pair = jnp.dot(mix[...], block, preferred_element_type=F32)
         comb = (pair[:TOK] + pair[TOK:]).astype(BF16).astype(F32).T
         ssq[...] += jnp.sum(comb * comb, axis=0, keepdims=True)
@@ -190,14 +222,35 @@
                     z_s.at[pl.ds(pl.multiple_of(t * 64, 64), 64)], z_r.at[z], zsend_sem, zrecv_sem, device_id={"dp": t}, device_id_type=MESH
                 ).start()
 
-    expert_part(0)
-
-    @pl.loop(1, 8)
+    @pl.loop(0, 8 + LAG)
     def _(k):
-        expert_part(k)
-        home_part(k - 1)
-
-    home_part(7)
+        @pl.when((k == 0) | (k == 4))
+        def _():
+            expert_rest(k // 4)
+
+        @pl.when(k < 8)
+        def _():
+            expert_main(k)
+
+        @pl.when((k == LAG) & (e == RELAY))
+        def _():
+            pl.semaphore_wait(bar, N - 1)
+
+            @pl.loop(1, N)
+            def _(d):
+                pl.semaphore_signal(open_sem, 1, device_id={"expert": e ^ d}, device_id_type=MESH)
+
+        @pl.when((k == LAG) & (e != RELAY))
+        def _():
+            pl.semaphore_wait(open_sem, 1)
+
+        @pl.when((k == LAG) | (k == LAG + 4))
+        def _():
+            home_rest((k - LAG) // 4)
+
+        @pl.when(k >= LAG)
+        def _():
+            home_main(k - LAG)
 
     inv_s[...] = lax.rsqrt(ssq[...] * (1.0 / D) + epsilon)
 
@@ -215,7 +268,7 @@
     column = jnp.sum(jnp.where(mine, line, 0.0), axis=1, keepdims=True)
 
     drain(send, CHUNKS * (N - 1), send_sem)
-    drain(ret_s, 8 * (N - 1), rsend_sem)
+    drain(ret_s, 10 * (N - 1), rsend_sem)
     drain(z_s, (N - 1) * 64, zsend_sem)
     drain(inv_r, N - 1, isend_sem)
     drain(z_r, N - 1, zrecv_sem)
@@ -245,18 +298,22 @@
             pltpu.VMEM((N * 16, 256), BF16),
             pltpu.VMEM((320, FF), F32),
             pltpu.VMEM((320, FF), F32),
-            pltpu.VMEM((N * 16, FF), BF16),
-            pltpu.VMEM((2 * TOK, N * 16), BF16),
-            pltpu.VMEM((8 * N, 16, QUAD), BF16),
-            pltpu.VMEM((8 * N, 16, QUAD), BF16),
+            pltpu.VMEM((320, FF), BF16),
+            pltpu.VMEM((2 * TOK, 320), BF16),
+            pltpu.VMEM((N * 16, N * 16), BF16),
+            pltpu.VMEM((N * 16, N * 16), BF16),
+            pltpu.VMEM((10 * N, 16, 128), BF16),
+            pltpu.VMEM((10 * N, 16, 128), BF16),
+            pltpu.VMEM((8, 64, 128), BF16),
             pltpu.VMEM((D, TOK), BF16),
             pltpu.VMEM((N, 64, TOK), BF16),
             pltpu.VMEM((1, TOK), F32),
             pltpu.VMEM((N, 1, TOK), F32),
             pltpu.VMEM((1, TOK), F32),
-            dma((7,)), dma, dma((CHUNKS,)), dma, dma((8,)), dma, dma, dma, dma,
+            dma((7,)), dma, dma((CHUNKS,)), dma, dma((10,)), dma, dma, dma, dma,
+            pltpu.SemaphoreType.REGULAR, pltpu.SemaphoreType.REGULAR,
         ],
-        compiler_params=pltpu.CompilerParams(collective_id=0, has_side_effects=True, vmem_limit_bytes=48 << 20),
+        compiler_params=pltpu.CompilerParams(collective_id=0, has_side_effects=True, vmem_limit_bytes=63 << 20),
         cost_estimate=pl.CostEstimate(flops=3 << 30, bytes_accessed=10 << 20, transcendentals=320 * FF),
     )(
         tokens[0],

time: 119 us -> 111 us (0.933)
  local copies, waits for them, and re-layouts: 6.36 us -> 1.87 us
  Pallas kernels: 112 us -> 109 us
    unnamed x13 -> x1, local copies, waits for them, and re-layouts: 6.36 us -> 1.87 us
    pallas_call x1, Pallas kernels: 112 us -> 109 us  [local(): pl.pallas_call(kernel, out_shape=jax.ShapeDtypeStruct((D // N, N * TOK),...]
where the time goes in v2:
time: 111 us; the launch traced here: 110 us
  Pallas kernels  109 us (98%)
  local copies, waits for them, and re-layouts  1.87 us (2%)
    pallas_call x1, Pallas kernels, local(): pl.pallas_call(kernel, out_shape=jax.ShapeDtypeStruct((D // N, N * TOK),...  109 us

profile of v2, /device:TPU:1, one launch (start us, length us, event | category | flops | bytes accessed | tf_op | source)
XLA Modules:
  0.0 110.4 jit_solution(16293977536761134132)
XLA Ops:
  0.0 108.5 %shard_map.82 = bf16[64,4096]{1,0:T(8,128)(2,1)} custom-call(bf16[128,2048]{1,0:T(8,128)(2,1)} %bitcast.22, s32[2,128]{1,0:T(2,128)} %bitcast.24, s32[2,128]{1,0:T(2,128)} %bitcast.25, f32[16]{0:T(128)} %table_ref.1, bf16[704,2048]{1,0:T(8,128)(2,1)} %bitcast.19, bf16[704,2048]{1,0:T(8,128)(2,1)} %bitcast.20, bf16[704,2048]{1,0:T(8,128)(2,1)} %bitcast.21, ...), custom_call_target="tpu_custom_call" | custom-call | flops 3221225472 | bytes 10485760 | tf_op jit(solution)/shard_map/pallas_call | solution.py:283
  108.6 1.9 %copy.10 = bf16[1,4096,64]{1,2,0:T(8,128)(2,1)} copy(bf16[1,4096,64]{1,2,0:T(8,128)(2,1)} %bitcast.18) | data formatting | bytes 1048576

commit v3 on v2

--- a/solution.py
+++ b/solution.py
@@ -22,6 +22,19 @@
 RELAY = 31
 LAG = 2
 CHUNKS = 5
+
+
+OFFSETS = sorted(((i, j) for i in range(4) for j in range(4)), key=lambda o: -min(o[0], 4 - o[0]) - min(o[1], 4 - o[1]))
+
+
+def plane_peers(e):
+    x, y, core = e // 8, (e // 2) % 4, e % 2
+    columns = [((x + i) % 4) * 8 for i in range(4)]
+    lines = [((y + j) % 4) * 2 for j in range(4)]
+    for i, j in OFFSETS:
+        if (i, j) != (0, 0):
+            yield columns[i] + lines[j] + core
+        yield columns[i] + lines[j] + 1 - core
 
 
 def drain(ref, count, sem):
@@ -113,15 +126,15 @@
         def _(d):
             pl.semaphore_signal(bar, 1, device_id={"dp": (z + d) % N}, device_id_type=MESH)
 
-    for c in (4, 0, 1, 2, 3):
-
-        @pl.loop(1, N)
-        def _(d):
-            t = e ^ d
+    peers = list(plane_peers(e))
+
+    @pl.loop(0, CHUNKS)
+    def _(i):
+        c = (i + 4) % CHUNKS
+        for t in peers:
             pltpu.make_async_remote_copy(
                 send.at[c * N + t], recv.at[c * N + e], send_sem, recv_sem.at[c], device_id={"expert": t}, device_id_type=MESH
             ).start()
-
         recv[c * N + e] = send[c * N + e]
 
     weight = [jnp.zeros((1, TOK), F32) for _ in range(2)]
@@ -173,9 +186,7 @@
     def give_back(at, block):
         ret_s[pl.ds(at * N, N)] = block.reshape(N, 16, 128).astype(BF16)
 
-        @pl.loop(1, N)
-        def _(d):
-            t = e ^ d
+        for t in peers:
             pltpu.make_async_remote_copy(
                 ret_s.at[at * N + t], ret_r.at[at * N + e], rsend_sem, rrecv_sem.at[at], device_id={"expert": t}, device_id_type=MESH
             ).start()

time: 111 us -> 109 us (0.982)
  Pallas kernels: 109 us -> 107 us
    pallas_call x1, Pallas kernels: 109 us -> 107 us  [local(): pl.pallas_call(kernel, out_shape=jax.ShapeDtypeStruct((D // N, N * TOK),...]
where the time goes in v3:
time: 109 us
  Pallas kernels  107 us (98%)
  local copies, waits for them, and re-layouts  1.87 us (2%)
    pallas_call x1, Pallas kernels, local(): pl.pallas_call(kernel, out_shape=jax.ShapeDtypeStruct((D // N, N * TOK),...  107 us

profile of v3, /device:TPU:1, one launch (start us, length us, event | category | flops | bytes accessed | tf_op | source)
XLA Modules:
  0.0 108.6 jit_solution(13420361697937953915)
XLA Ops:
  0.0 106.7 %shard_map.82 = bf16[64,4096]{1,0:T(8,128)(2,1)} custom-call(bf16[128,2048]{1,0:T(8,128)(2,1)} %bitcast.22, s32[2,128]{1,0:T(2,128)} %bitcast.24, s32[2,128]{1,0:T(2,128)} %bitcast.25, f32[16]{0:T(128)} %table_ref.1, bf16[704,2048]{1,0:T(8,128)(2,1)} %bitcast.19, bf16[704,2048]{1,0:T(8,128)(2,1)} %bitcast.20, bf16[704,2048]{1,0:T(8,128)(2,1)} %bitcast.21, ...), custom_call_target="tpu_custom_call" | custom-call | flops 3221225472 | bytes 10485760 | tf_op jit(solution)/shard_map/pallas_call | solution.py:294
  106.7 1.9 %copy.10 = bf16[1,4096,64]{1,2,0:T(8,128)(2,1)} copy(bf16[1,4096,64]{1,2,0:T(8,128)(2,1)} %bitcast.18) | data formatting | bytes 1048576

commit v4 on v3

--- a/solution.py
+++ b/solution.py
@@ -235,13 +235,13 @@
 
     @pl.loop(0, 8 + LAG)
     def _(k):
+        @pl.when(k < 8)
+        def _():
+            expert_main(k)
+
         @pl.when((k == 0) | (k == 4))
         def _():
             expert_rest(k // 4)
-
-        @pl.when(k < 8)
-        def _():
-            expert_main(k)
 
         @pl.when((k == LAG) & (e == RELAY))
         def _():

time: 109 us -> 109 us (level)
  no operation moved by 1% of the time
where the time goes in v4:
time: 109 us
  Pallas kernels  107 us (98%)
  local copies, waits for them, and re-layouts  1.87 us (2%)
    pallas_call x1, Pallas kernels, local(): pl.pallas_call(kernel, out_shape=jax.ShapeDtypeStruct((D // N, N * TOK),...  107 us

profile of v4, /device:TPU:1, one launch (start us, length us, event | category | flops | bytes accessed | tf_op | source)
XLA Modules:
  0.0 109.1 jit_solution(11962225389716812116)
XLA Ops:
  0.0 107.2 %shard_map.82 = bf16[64,4096]{1,0:T(8,128)(2,1)} custom-call(bf16[128,2048]{1,0:T(8,128)(2,1)} %bitcast.22, s32[2,128]{1,0:T(2,128)} %bitcast.24, s32[2,128]{1,0:T(2,128)} %bitcast.25, f32[16]{0:T(128)} %table_ref.1, bf16[704,2048]{1,0:T(8,128)(2,1)} %bitcast.19, bf16[704,2048]{1,0:T(8,128)(2,1)} %bitcast.20, bf16[704,2048]{1,0:T(8,128)(2,1)} %bitcast.21, ...), custom_call_target="tpu_custom_call" | custom-call | flops 3221225472 | bytes 10485760 | tf_op jit(solution)/shard_map/pallas_call | solution.py:294
  107.2 1.9 %copy.10 = bf16[1,4096,64]{1,2,0:T(8,128)(2,1)} copy(bf16[1,4096,64]{1,2,0:T(8,128)(2,1)} %bitcast.18) | data formatting | bytes 1048576
